TPU v7x, 512 devices: a whole 4x8x8 slice. The times are simulated.
512 devices in a mesh: tm: 128 (over z_lo, x, y, core), series: 4 (over z_hi).
Axes of the slice: x: 4, y: 8, z: 8 (z_hi: 4, z_lo: 2; z = z_hi * 2 + z_lo), core: 2. Of those that a mesh axis runs over, the one named last changes fastest.
Arguments:
- time_query: bfloat16 [20, 8192, 512], P('series', 'tm'), may hold values from -160 to 160
- time_key: bfloat16 [20, 8192, 512], P('series', 'tm'), may hold values from -6 to 6
- time_value: bfloat16 [20, 8192, 512], P('series', 'tm'), may hold values from -6 to 6
- group_query: bfloat16 [20, 8192, 512], P('series', 'tm'), may hold values from -160 to 160
- group_key: bfloat16 [20, 8192, 512], P('series', 'tm'), may hold values from -6 to 6
- group_value: bfloat16 [20, 8192, 512], P('series', 'tm'), may hold values from -6 to 6
- out_time: bfloat16 [512, 768], P('series'), may hold values from -0.25 to 0.25
- out_group: bfloat16 [512, 768], P('series'), may hold values from -0.25 to 0.25
- series_group: int32 [20], replicated, may hold values from 0 to 1, as said below
- band_width: int32 [8], replicated, may hold values from 2 to 16, as said below
- cotangent: bfloat16 [20, 8192, 768], P('series', 'tm'), may hold values from -6 to 6
Outputs:
- grad_time_query: bfloat16 [20, 8192, 512], P('series', 'tm')
- grad_time_key: bfloat16 [20, 8192, 512], P('series', 'tm')
- grad_time_value: bfloat16 [20, 8192, 512], P('series', 'tm')
- grad_group_query: bfloat16 [20, 8192, 512], P('series', 'tm')
- grad_group_key: bfloat16 [20, 8192, 512], P('series', 'tm')
- grad_group_value: bfloat16 [20, 8192, 512], P('series', 'tm')
- grad_out_time: float32 [512, 768], P('series', 'tm')
- grad_out_group: float32 [512, 768], P('series', 'tm')
Inputs may be any that keep to these rules, and one draw needn't show every extreme that they name: `series_group`: series with equal numbers form one group; there are two groups, one of exactly 16 series and one of exactly 4. `band_width`: some head's band is exactly 16.
All inputs are finite; a program needn't handle non-finite values.
Results may differ from a plain program's by a relative error of at most 0.0058.
Values may be sent and summed in bfloat16 or wider, within the bound.
No kernel may reach another device: no remote copies, remote signals or barrier semaphores. Data moves between devices by JAX's collectives and lax.ppermute only.
A program may use at most 128 MiB of HBM per device.

v0:
```python
import jax
import jax.numpy as jnp
from jax import lax
from jax.sharding import PartitionSpec as P

HEAD_DIM = 64
BAND = 16
masked_score = -1e30


def passed_along(value, axis, steps):
    count = lax.axis_size(axis)
    leading, last = (max(0, -steps), min(count, count - steps))
    return lax.ppermute(value, axis, [(source, source + steps) for source in range(leading, last)])


def soft_weights(scores, keep_mask):
    scores = jnp.where(keep_mask, scores, masked_score)
    row_top = jnp.max(scores, axis=-1, keepdims=True)
    weights = jnp.exp(scores - row_top)
    return weights / jnp.sum(weights, axis=-1, keepdims=True)


def score_grad(probabilities, grad_prob, score_scale):
    grad_inner = lax.optimization_barrier(grad_prob.astype(jnp.bfloat16)).astype(jnp.float32)
    centred = grad_inner - jnp.sum(grad_inner * probabilities, axis=-1, keepdims=True)
    return probabilities * centred * score_scale


def temporal_attend(query_rows, key_ext, value_ext, out_grad, band_width, first_row):
    ser_count, block_rows, row_width = query_rows.shape
    head_count = band_width.shape[0]
    head_depth = row_width // head_count
    border_rows = key_ext.shape[1] - block_rows
    score_scale = head_depth ** (-0.5)
    query_heads = query_rows.reshape(ser_count, block_rows, head_count, head_depth)
    key_heads = key_ext.reshape(ser_count, block_rows + border_rows, head_count, head_depth)
    value_heads = value_ext.reshape(ser_count, block_rows + border_rows, head_count, head_depth)
    grad_heads = out_grad.reshape(ser_count, block_rows, head_count, head_depth)
    scores = (
        jnp.einsum("sthd,sihd->shti", query_heads, key_heads, preferred_element_type=jnp.float32)
        * score_scale
    )
    query_pos = lax.broadcasted_iota(jnp.int32, (block_rows, block_rows + border_rows), 0)
    key_pos = lax.broadcasted_iota(jnp.int32, (block_rows, block_rows + border_rows), 1)
    offset = query_pos + border_rows - key_pos
    absolute = first_row + key_pos - border_rows
    in_band = (
        (offset[None] >= 0) & (offset[None] < band_width[:, None, None]) & (absolute[None] >= 0)
    )
    probabilities = soft_weights(scores, in_band[None])
    rounded = probabilities.astype(jnp.bfloat16)
    mixed_out = jnp.einsum(
        "shti,sihd->sthd", rounded, value_heads, preferred_element_type=jnp.float32
    )
    grad_value = jnp.einsum(
        "shti,sthd->sihd", rounded, grad_heads, preferred_element_type=jnp.float32
    )
    grad_prob = jnp.einsum(
        "sthd,sihd->shti", grad_heads, value_heads, preferred_element_type=jnp.float32
    )
    grad_score = score_grad(probabilities, grad_prob, score_scale)
    grad_query = jnp.einsum(
        "shti,sihd->sthd",
        grad_score,
        key_heads.astype(jnp.float32),
        precision=lax.Precision.HIGHEST,
    )
    grad_key = jnp.einsum(
        "shti,sthd->sihd",
        grad_score,
        query_heads.astype(jnp.float32),
        precision=lax.Precision.HIGHEST,
    )
    ext_rows = block_rows + border_rows
    return (
        mixed_out.reshape(ser_count, block_rows, row_width),
        grad_query.reshape(ser_count, block_rows, row_width),
        grad_key.reshape(ser_count, ext_rows, row_width),
        grad_value.reshape(ser_count, ext_rows, row_width),
    )


def group_attend(query_rows, key_rows, value_rows, out_grad, series_group):
    ser_count, block_rows, row_width = query_rows.shape
    head_count = row_width // HEAD_DIM
    score_scale = HEAD_DIM ** (-0.5)
    query_heads = query_rows.reshape(ser_count, block_rows, head_count, HEAD_DIM)
    key_heads = key_rows.reshape(ser_count, block_rows, head_count, HEAD_DIM)
    value_heads = value_rows.reshape(ser_count, block_rows, head_count, HEAD_DIM)
    grad_heads = out_grad.reshape(ser_count, block_rows, head_count, HEAD_DIM)
    scores = (
        jnp.einsum("sthd,rthd->thsr", query_heads, key_heads, preferred_element_type=jnp.float32)
        * score_scale
    )
    same_group = series_group[:, None] == series_group[None, :]
    probabilities = soft_weights(scores, same_group[None, None])
    rounded = probabilities.astype(jnp.bfloat16)
    mixed_out = jnp.einsum(
        "thsr,rthd->sthd", rounded, value_heads, preferred_element_type=jnp.float32
    )
    grad_value = jnp.einsum(
        "thsr,sthd->rthd", rounded, grad_heads, preferred_element_type=jnp.float32
    )
    grad_prob = jnp.einsum(
        "sthd,rthd->thsr", grad_heads, value_heads, preferred_element_type=jnp.float32
    )
    grad_score = score_grad(probabilities, grad_prob, score_scale)
    grad_query = jnp.einsum(
        "thsr,rthd->sthd",
        grad_score,
        key_heads.astype(jnp.float32),
        precision=lax.Precision.HIGHEST,
    )
    grad_key = jnp.einsum(
        "thsr,sthd->rthd",
        grad_score,
        query_heads.astype(jnp.float32),
        precision=lax.Precision.HIGHEST,
    )
    out_shape = (ser_count, block_rows, row_width)
    return (
        mixed_out.reshape(out_shape),
        grad_query.reshape(out_shape),
        grad_key.reshape(out_shape),
        grad_value.reshape(out_shape),
    )


def group_local(moved_parts, series_group):
    query_rows, key_rows, value_rows, out_grad = moved_parts
    mixed_out, grad_query, grad_key, grad_value = group_attend(
        query_rows, key_rows, value_rows, out_grad, series_group
    )
    return (
        mixed_out.astype(jnp.bfloat16),
        grad_query.astype(jnp.bfloat16),
        grad_key.astype(jnp.bfloat16),
        grad_value.astype(jnp.bfloat16),
    )


def per_device(
    time_query,
    time_key,
    time_value,
    group_query,
    group_key,
    group_value,
    out_time,
    out_group,
    series_group,
    band_width,
    cotangent,
):
    ser_dev, block_rows, row_width = time_query.shape
    border_rows = BAND - 1
    w_time, w_group = (
        lax.all_gather(out_time, "series", axis=0, tiled=True),
        lax.all_gather(out_group, "series", axis=0, tiled=True),
    )
    cot_flat = cotangent.reshape(-1, cotangent.shape[2])

    def back_project(weight):
        product = lax.dot_general(
            cot_flat, weight, (((1,), (1,)), ((), ())), preferred_element_type=jnp.float32
        )
        return product.astype(jnp.bfloat16).reshape(ser_dev, block_rows, row_width)

    d_time = back_project(w_time)
    d_group = back_project(w_group)
    rim_key, rim_value = passed_along(
        (time_key[:, block_rows - border_rows :], time_value[:, block_rows - border_rows :]),
        "tm",
        1,
    )
    key_ext = jnp.concatenate([rim_key, time_key], axis=1)
    value_ext = jnp.concatenate([rim_value, time_value], axis=1)
    first_row = lax.axis_index("tm") * block_rows
    temporal_mixture, temporal_query_gradient, extended_key_gradient, extended_value_gradient = (
        temporal_attend(time_query, key_ext, value_ext, d_time, band_width, first_row)
    )
    time_out = temporal_mixture.astype(jnp.bfloat16)
    pulled_key_rows, pulled_value_rows = passed_along(
        (extended_key_gradient[:, :border_rows], extended_value_gradient[:, :border_rows]), "tm", -1
    )
    empty_padding_rows = jnp.zeros((ser_dev, block_rows - border_rows, row_width), jnp.float32)
    grad_tk = (
        extended_key_gradient[:, border_rows:]
        + jnp.concatenate([empty_padding_rows, pulled_key_rows], axis=1)
    ).astype(jnp.bfloat16)
    temporal_value_gradient = (
        extended_value_gradient[:, border_rows:]
        + jnp.concatenate([empty_padding_rows, pulled_value_rows], axis=1)
    ).astype(jnp.bfloat16)
    temporal_query_gradient = temporal_query_gradient.astype(jnp.bfloat16)
    moved_parts = (
        lax.all_to_all(group_query, "series", split_axis=1, concat_axis=0, tiled=True),
        lax.all_to_all(group_key, "series", split_axis=1, concat_axis=0, tiled=True),
        lax.all_to_all(group_value, "series", split_axis=1, concat_axis=0, tiled=True),
        lax.all_to_all(d_group, "series", split_axis=1, concat_axis=0, tiled=True),
    )
    results = group_local(moved_parts, series_group)
    group_out, grad_gq, grad_gk, grad_gv = (
        lax.all_to_all(results[0], "series", split_axis=0, concat_axis=1, tiled=True),
        lax.all_to_all(results[1], "series", split_axis=0, concat_axis=1, tiled=True),
        lax.all_to_all(results[2], "series", split_axis=0, concat_axis=1, tiled=True),
        lax.all_to_all(results[3], "series", split_axis=0, concat_axis=1, tiled=True),
    )
    grad_scale = (ser_dev * block_rows * lax.axis_size("series") * lax.axis_size("tm")) ** (-0.5)
    term_time = (
        lax.dot_general(
            time_out.reshape(-1, row_width),
            cot_flat,
            (((0,), (0,)), ((), ())),
            preferred_element_type=jnp.float32,
        )
        * grad_scale
    )
    term_group = (
        lax.dot_general(
            group_out.reshape(-1, row_width),
            cot_flat,
            (((0,), (0,)), ((), ())),
            preferred_element_type=jnp.float32,
        )
        * grad_scale
    )
    partial_sums = (
        lax.psum_scatter(term_time, "tm", scatter_dimension=1, tiled=True),
        lax.psum_scatter(term_group, "tm", scatter_dimension=1, tiled=True),
    )
    grad_wt, grad_wg = (
        lax.psum_scatter(partial_sums[0], "series", scatter_dimension=0, tiled=True),
        lax.psum_scatter(partial_sums[1], "series", scatter_dimension=0, tiled=True),
    )
    return (
        temporal_query_gradient,
        grad_tk,
        temporal_value_gradient,
        grad_gq,
        grad_gk,
        grad_gv,
        grad_wt,
        grad_wg,
    )


def solution(mesh):
    placed = (
        P("series", "tm", None),
        P("series", "tm", None),
        P("series", "tm", None),
        P("series", "tm", None),
        P("series", "tm", None),
        P("series", "tm", None),
        P("series", None),
        P("series", None),
        P(),
        P(),
        P("series", "tm", None),
    )
    return jax.shard_map(
        per_device,
        mesh=mesh,
        in_specs=placed,
        out_specs=(
            P("series", "tm", None),
            P("series", "tm", None),
            P("series", "tm", None),
            P("series", "tm", None),
            P("series", "tm", None),
            P("series", "tm", None),
            P("series", "tm"),
            P("series", "tm"),
        ),
        check_vma=False,
    )
```

profile of v0, /device:TPU:2, one launch (start us, length us, event | category | flops | bytes accessed | tf_op | source)
XLA Modules:
  0.0 800.1 jit_solution(5145301826097418971)
XLA Ops:
  11.1 19.1 %collective-permute-start.1 = (bf16[5,15,512]{2,1,0:T(8,128)(2,1)S(1)}, bf16[5,15,512]{2,1,0:T(8,128)(2,1)S(1)}, u32[]{:S(2)}, u32[]{:S(2)}) collective-permute-start(bf16[5,15,512]{2,1,0:T(8,128)(2,1)S(1)} %slice.19), channel_id=1, source_target_pairs={{0,4},{4,8},{8,12},{12,16},{16,20},{20,24},{24,28},{28,32},{32,36}... | collective-permute-start | bytes 230408 | tf_op jit(solution)/shard_map/ppermute | solution.py:14
  32.1 8.7 %all-to-all-start.3 = ((bf16[5,64,512]{2,0,1:T(8,128)(2,1)}), bf16[5,64,512]{2,0,1:T(8,128)(2,1)}, u32[]{:S(2)}, u32[]{:S(2)}) async-start(bf16[5,64,512]{2,0,1:T(8,128)(2,1)} %copy.160), calls=%async_computation.3 | async-start | bytes 1048576 | tf_op jit(solution)/shard_map/all_to_all | solution.py:200
  41.0 30.3 %all_gather.6 = bf16[512,768]{1,0:T(8,128)(2,1)S(1)} all-gather(bf16[128,768]{1,0:T(8,128)(2,1)S(1)} %copy-done.27), channel_id=1, replica_groups=mesh['tm'=128,'series'=4] {'series'}, dimensions={0}, use_global_device_ids=true | all-gather | bytes 983040 | tf_op jit(solution)/shard_map/all_gather | solution.py:159
  71.3 17.7 %all_gather.7 = bf16[512,768]{1,0:T(8,128)(2,1)S(1)} all-gather(bf16[128,768]{1,0:T(8,128)(2,1)S(1)} %copy-done.28), channel_id=1, replica_groups=mesh['tm'=128,'series'=4] {'series'}, dimensions={0}, use_global_device_ids=true | all-gather | bytes 983040 | tf_op jit(solution)/shard_map/all_gather | solution.py:160
  96.9 5.6 all-to-all-start.1
  104.0 6.9 fusion.53
  110.9 4.6 all-to-all-done.1
  115.5 4.1 all-to-all-start
  135.0 3.3 copy.156
  143.1 5.7 all-to-all-start.7
  148.7 7.3 convolution_convert_fusion.5
  156.0 3.1 bitcast_multiply_fusion
  161.5 4.8 all-to-all-start.2
  168.1 269.2 %fusion.52 = (f32[512,8]{0,1:T(8,128)S(1)}, f32[512,8]{0,1:T(8,128)S(1)}) fusion(f32[512,768]{0,1:T(8,128)} %bitcast_multiply_fusion, f32[512,768]{0,1:T(8,128)} %convolution_multiply_fusion), kind=kCustom, calls=%all-reduce-scatter.2 | all-reduce-scatter fusion | flops 1048577 | bytes 3180544
  438.6 12.3 %collective-permute-start.33 = (f32[512,8]{0,1:T(8,128)S(1)}, f32[512,8]{0,1:T(8,128)S(1)}, u32[]{:S(2)}, u32[]{:S(2)}) collective-permute-start(f32[512,8]{0,1:T(8,128)S(1)} %get-tuple-element.50), channel_id=1, source_target_pairs={{0,120},{4,124},{8,128},{12,132},{16,136},{20,140},{24,144},{28,14... | collective-permute-start | bytes 49160
  450.9 7.8 collective-permute-start.32
  461.5 18.1 %collective-permute-start.31 = (f32[512,8]{0,1:T(8,128)S(1)}, f32[512,8]{0,1:T(8,128)S(1)}, u32[]{:S(2)}, u32[]{:S(2)}) collective-permute-start(f32[512,8]{0,1:T(8,128)S(1)} %get-tuple-element.50), channel_id=1, source_target_pairs={{0,112},{4,116},{8,120},{12,124},{16,128},{20,132},{24,136},{28,14... | collective-permute-start | bytes 49160
  479.6 10.9 %collective-permute-start.30 = (f32[512,8]{0,1:T(8,128)S(1)}, f32[512,8]{0,1:T(8,128)S(1)}, u32[]{:S(2)}, u32[]{:S(2)}) collective-permute-start(f32[512,8]{0,1:T(8,128)S(1)} %get-tuple-element.50), channel_id=1, source_target_pairs={{0,108},{4,112},{8,116},{12,120},{16,124},{20,128},{24,132},{28,13... | collective-permute-start | bytes 49160
  490.6 17.6 %collective-permute-start.29 = (f32[512,8]{0,1:T(8,128)S(1)}, f32[512,8]{0,1:T(8,128)S(1)}, u32[]{:S(2)}, u32[]{:S(2)}) collective-permute-start(f32[512,8]{0,1:T(8,128)S(1)} %get-tuple-element.50), channel_id=1, source_target_pairs={{0,104},{4,108},{8,112},{12,116},{16,120},{20,124},{24,128},{28,13... | collective-permute-start | bytes 49160
  510.1 3.1 collective-permute-start.27
  519.2 4.5 collective-permute-start.22
  523.7 3.0 collective-permute-start.21
  530.7 3.8 collective-permute-start.18
  541.3 3.1 collective-permute-start.15
  546.9 3.0 collective-permute-start.13
  550.0 4.1 collective-permute-start.12
  555.1 4.2 collective-permute-start.11
  561.3 4.0 collective-permute-start.9
  565.4 3.8 collective-permute-start.8
  571.6 14.8 %fusion.10 = f32[16,8,20,20]{3,1,2,0:T(8,128)} fusion(bf16[16,8,20,20]{3,1,2,0:T(8,128)(2,1)S(1)} %copy.214, f32[16,8,20,20]{3,1,2,0:T(8,128)S(1)} %copy-done.9, f32[16,8,20]{1,2,0:T(8,128)S(1)} %copy-done.21), kind=kOutput, calls=%fused_computation.14 | output fusion | flops 412179 | bytes 522240 | tf_op jit(solution)/shard_map/sub | solution.py:26
  588.7 3.4 collective-permute-start.6
  598.9 2.9 fusion.18
  605.0 5.0 all-to-all-start.4
  619.6 4.2 convolution_convert_fusion.4
  637.2 7.1 all-to-all-start.5
  652.0 3.0 collective-permute-start.50
  655.0 7.3 fusion.45
  682.0 3.2 collective-permute-start.45
  687.5 7.1 all-to-all-start.6
  694.6 3.5 collective-permute-start.44
  698.1 3.1 collective-permute-start.43
  703.2 3.6 collective-permute-start.41
  706.7 3.4 collective-permute-start.40
  711.2 8.1 %concatenate.16 = f32[512,262]{0,1:T(8,128)S(1)} concatenate(f32[512,6]{0,1:T(8,128)S(1)} %copy-done.41, f32[512,8]{0,1:T(8,128)S(1)} %copy-done.35, f32[512,8]{0,1:T(8,128)S(1)} %copy-done.37, f32[512,8]{0,1:T(8,128)S(1)} %copy-done.39, f32[512,8]{0,1:T(8,128)S(1)} %copy-done.43, f32[512,8]{0,1:T(8,128)S(1)} %copy-done.45, f32[512,8]{0,1:T(8,128)S(1)} %copy-done.47, ...), dimensions={1} | concatenate | bytes 1073152
  719.4 6.1 collective-permute-start.3
  739.1 9.6 %concatenate.17 = f32[512,262]{0,1:T(8,128)S(1)} concatenate(f32[512,6]{0,1:T(8,128)S(1)} %copy-done.33, f32[512,8]{0,1:T(8,128)S(1)} %copy-done.73, f32[512,8]{0,1:T(8,128)S(1)} %copy-done.75, f32[512,8]{0,1:T(8,128)S(1)} %copy-done.83, f32[512,8]{0,1:T(8,128)S(1)} %copy-done.87, f32[512,8]{0,1:T(8,128)S(1)} %copy-done.91, f32[512,8]{0,1:T(8,128)S(1)} %copy-done.93, ...), dimensions={1} | concatenate | bytes 1073152
  753.3 10.1 %reduce-scatter.7.cloned.1.call-done = f32[128,6]{0,1:T(8,128)} async-done(((f32[512,6]{0,1:T(8,128)}), f32[128,6]{0,1:T(8,128)}) %reduce-scatter.7.cloned.1.call-update) | async-done | bytes 3088 | tf_op jit(solution)/shard_map/reduce_scatter | solution.py:234
  763.4 29.6 %reduce-scatter.9.cloned.1.call-done = f32[128,6]{0,1:T(8,128)} async-done(((f32[512,6]{0,1:T(8,128)}), f32[128,6]{0,1:T(8,128)}) %reduce-scatter.9.cloned.1.call-update) | async-done | bytes 3088 | tf_op jit(solution)/shard_map/reduce_scatter | solution.py:235
  (400 shorter events, 153.6 us)
Async XLA Ops:
  8.2 86.9 %collective-permute-start = (bf16[5,15,512]{2,1,0:T(8,128)(2,1)S(1)}, bf16[5,15,512]{2,1,0:T(8,128)(2,1)S(1)}, u32[]{:S(2)}, u32[]{:S(2)}) collective-permute-start(bf16[5,15,512]{2,1,0:T(8,128)(2,1)S(1)} %slice.18), channel_id=1, source_target_pairs={{0,4},{4,8},{8,12},{12,16},{16,20},{20,24},{24,28},{28,32},{32,36}... | collective-permute-start | bytes 230408 | tf_op jit(solution)/shard_map/ppermute | solution.py:14
  11.1 84.5 %collective-permute-start.1 = (bf16[5,15,512]{2,1,0:T(8,128)(2,1)S(1)}, bf16[5,15,512]{2,1,0:T(8,128)(2,1)S(1)}, u32[]{:S(2)}, u32[]{:S(2)}) collective-permute-start(bf16[5,15,512]{2,1,0:T(8,128)(2,1)S(1)} %slice.19), channel_id=1, source_target_pairs={{0,4},{4,8},{8,12},{12,16},{16,20},{20,24},{24,28},{28,32},{32,36}... | collective-permute-start | bytes 230408 | tf_op jit(solution)/shard_map/ppermute | solution.py:14
  32.1 64.3 %all-to-all-start.3 = ((bf16[5,64,512]{2,0,1:T(8,128)(2,1)}), bf16[5,64,512]{2,0,1:T(8,128)(2,1)}, u32[]{:S(2)}, u32[]{:S(2)}) async-start(bf16[5,64,512]{2,0,1:T(8,128)(2,1)} %copy.160), calls=%async_computation.3 | async-start | bytes 1048576 | tf_op jit(solution)/shard_map/all_to_all | solution.py:200
  124.2 335.9 %collective-permute-start.2 = (f32[5,15,512]{2,1,0:T(8,128)}, f32[5,15,512]{2,1,0:T(8,128)S(1)}, u32[]{:S(2)}, u32[]{:S(2)}) collective-permute-start(f32[5,15,512]{2,1,0:T(8,128)} %copy.186), channel_id=1, source_target_pairs={{4,0},{8,4},{12,8},{16,12},{20,16},{24,20},{28,24},{32,28},{36,32}... | collective-permute-start | bytes 460808 | tf_op jit(solution)/shard_map/ppermute | solution.py:14
  161.5 377.2 %all-to-all-start.2 = ((bf16[5,64,512]{2,0,1:T(8,128)(2,1)}), bf16[5,64,512]{2,0,1:T(8,128)(2,1)S(1)}, u32[]{:S(2)}, u32[]{:S(2)}) async-start(bf16[5,64,512]{2,0,1:T(8,128)(2,1)} %copy.157), calls=%async_computation.2 | async-start | bytes 1048576 | tf_op jit(solution)/shard_map/all_to_all | solution.py:201
  437.3 53.3 %collective-permute-start.34 = (f32[512,8]{0,1:T(8,128)S(1)}, f32[512,8]{0,1:T(8,128)S(1)}, u32[]{:S(2)}, u32[]{:S(2)}) collective-permute-start(f32[512,8]{0,1:T(8,128)S(1)} %get-tuple-element.50), channel_id=1, source_target_pairs={{0,124},{4,128},{8,132},{12,136},{16,140},{20,144},{24,148},{28,15... | collective-permute-start | bytes 49160
  438.6 69.6 %collective-permute-start.33 = (f32[512,8]{0,1:T(8,128)S(1)}, f32[512,8]{0,1:T(8,128)S(1)}, u32[]{:S(2)}, u32[]{:S(2)}) collective-permute-start(f32[512,8]{0,1:T(8,128)S(1)} %get-tuple-element.50), channel_id=1, source_target_pairs={{0,120},{4,124},{8,128},{12,132},{16,136},{20,140},{24,144},{28,14... | collective-permute-start | bytes 49160
  450.9 59.2 %collective-permute-start.32 = (f32[512,8]{0,1:T(8,128)S(1)}, f32[512,8]{0,1:T(8,128)S(1)}, u32[]{:S(2)}, u32[]{:S(2)}) collective-permute-start(f32[512,8]{0,1:T(8,128)S(1)} %get-tuple-element.50), channel_id=1, source_target_pairs={{0,116},{4,120},{8,124},{12,128},{16,132},{20,136},{24,140},{28,14... | collective-permute-start | bytes 49160
  460.1 19.5 %collective-permute-start.67 = (f32[512,6]{0,1:T(8,128)S(1)}, f32[512,6]{0,1:T(8,128)S(1)}, u32[]{:S(2)}, u32[]{:S(2)}) collective-permute-start(f32[512,6]{0,1:T(8,128)S(1)} %slice.29), channel_id=1, source_target_pairs={{0,128},{4,132},{8,136},{12,140},{16,144},{20,148},{24,152},{28,15... | collective-permute-start | bytes 36872
  461.5 51.7 %collective-permute-start.31 = (f32[512,8]{0,1:T(8,128)S(1)}, f32[512,8]{0,1:T(8,128)S(1)}, u32[]{:S(2)}, u32[]{:S(2)}) collective-permute-start(f32[512,8]{0,1:T(8,128)S(1)} %get-tuple-element.50), channel_id=1, source_target_pairs={{0,112},{4,116},{8,120},{12,124},{16,128},{20,132},{24,136},{28,14... | collective-permute-start | bytes 49160
  479.6 35.0 %collective-permute-start.30 = (f32[512,8]{0,1:T(8,128)S(1)}, f32[512,8]{0,1:T(8,128)S(1)}, u32[]{:S(2)}, u32[]{:S(2)}) collective-permute-start(f32[512,8]{0,1:T(8,128)S(1)} %get-tuple-element.50), channel_id=1, source_target_pairs={{0,108},{4,112},{8,116},{12,120},{16,124},{20,128},{24,132},{28,13... | collective-permute-start | bytes 49160
  490.6 25.3 %collective-permute-start.29 = (f32[512,8]{0,1:T(8,128)S(1)}, f32[512,8]{0,1:T(8,128)S(1)}, u32[]{:S(2)}, u32[]{:S(2)}) collective-permute-start(f32[512,8]{0,1:T(8,128)S(1)} %get-tuple-element.50), channel_id=1, source_target_pairs={{0,104},{4,108},{8,112},{12,116},{16,120},{20,124},{24,128},{28,13... | collective-permute-start | bytes 49160
  550.0 19.2 %collective-permute-start.12 = (f32[512,8]{0,1:T(8,128)S(1)}, f32[512,8]{0,1:T(8,128)S(1)}, u32[]{:S(2)}, u32[]{:S(2)}) collective-permute-start(f32[512,8]{0,1:T(8,128)S(1)} %get-tuple-element.50), channel_id=1, source_target_pairs={{0,36},{4,40},{8,44},{12,48},{16,52},{20,56},{24,60},{28,64},{32,6... | collective-permute-start | bytes 49160
  555.1 33.6 %collective-permute-start.11 = (f32[512,8]{0,1:T(8,128)S(1)}, f32[512,8]{0,1:T(8,128)S(1)}, u32[]{:S(2)}, u32[]{:S(2)}) collective-permute-start(f32[512,8]{0,1:T(8,128)S(1)} %get-tuple-element.50), channel_id=1, source_target_pairs={{0,32},{4,36},{8,40},{12,44},{16,48},{20,52},{24,56},{28,60},{32,6... | collective-permute-start | bytes 49160
  559.4 32.7 %collective-permute-start.10 = (f32[512,8]{0,1:T(8,128)S(1)}, f32[512,8]{0,1:T(8,128)S(1)}, u32[]{:S(2)}, u32[]{:S(2)}) collective-permute-start(f32[512,8]{0,1:T(8,128)S(1)} %get-tuple-element.50), channel_id=1, source_target_pairs={{0,28},{4,32},{8,36},{12,40},{16,44},{20,48},{24,52},{28,56},{32,6... | collective-permute-start | bytes 49160
  561.3 32.7 %collective-permute-start.9 = (f32[512,8]{0,1:T(8,128)S(1)}, f32[512,8]{0,1:T(8,128)S(1)}, u32[]{:S(2)}, u32[]{:S(2)}) collective-permute-start(f32[512,8]{0,1:T(8,128)S(1)} %get-tuple-element.50), channel_id=1, source_target_pairs={{0,24},{4,28},{8,32},{12,36},{16,40},{20,44},{24,48},{28,52},{32,5... | collective-permute-start | bytes 49160
  565.4 30.9 %collective-permute-start.8 = (f32[512,8]{0,1:T(8,128)S(1)}, f32[512,8]{0,1:T(8,128)S(1)}, u32[]{:S(2)}, u32[]{:S(2)}) collective-permute-start(f32[512,8]{0,1:T(8,128)S(1)} %get-tuple-element.50), channel_id=1, source_target_pairs={{0,20},{4,24},{8,28},{12,32},{16,36},{20,40},{24,44},{28,48},{32,5... | collective-permute-start | bytes 49160
  569.2 28.4 %collective-permute-start.7 = (f32[512,8]{0,1:T(8,128)S(1)}, f32[512,8]{0,1:T(8,128)S(1)}, u32[]{:S(2)}, u32[]{:S(2)}) collective-permute-start(f32[512,8]{0,1:T(8,128)S(1)} %get-tuple-element.50), channel_id=1, source_target_pairs={{0,16},{4,20},{8,24},{12,28},{16,32},{20,36},{24,40},{28,44},{32,4... | collective-permute-start | bytes 49160
  588.7 21.3 %collective-permute-start.6 = (f32[512,8]{0,1:T(8,128)S(1)}, f32[512,8]{0,1:T(8,128)S(1)}, u32[]{:S(2)}, u32[]{:S(2)}) collective-permute-start(f32[512,8]{0,1:T(8,128)S(1)} %get-tuple-element.50), channel_id=1, source_target_pairs={{0,12},{4,16},{8,20},{12,24},{16,28},{20,32},{24,36},{28,40},{32,4... | collective-permute-start | bytes 49160
  592.1 19.8 %collective-permute-start.5 = (f32[512,8]{0,1:T(8,128)S(1)}, f32[512,8]{0,1:T(8,128)}, u32[]{:S(2)}, u32[]{:S(2)}) collective-permute-start(f32[512,8]{0,1:T(8,128)S(1)} %get-tuple-element.50), channel_id=1, source_target_pairs={{0,8},{4,12},{8,16},{12,20},{16,24},{20,28},{24,32},{28,36},{32,40... | collective-permute-start | bytes 49160
  594.0 19.8 %collective-permute-start.4 = (f32[512,8]{0,1:T(8,128)S(1)}, f32[512,8]{0,1:T(8,128)}, u32[]{:S(2)}, u32[]{:S(2)}) collective-permute-start(f32[512,8]{0,1:T(8,128)S(1)} %get-tuple-element.50), channel_id=1, source_target_pairs={{0,4},{4,8},{8,12},{12,16},{16,20},{20,24},{24,28},{28,32},{32,36}... | collective-permute-start | bytes 49160
  597.6 20.0 %collective-permute-start.65 = (f32[512,8]{0,1:T(8,128)S(1)}, f32[512,8]{0,1:T(8,128)S(1)}, u32[]{:S(2)}, u32[]{:S(2)}) collective-permute-start(f32[512,8]{0,1:T(8,128)S(1)} %get-tuple-element.51), channel_id=1, source_target_pairs={{0,120},{4,124},{8,128},{12,132},{16,136},{20,140},{24,144},{28,14... | collective-permute-start | bytes 49160
  605.0 32.1 %all-to-all-start.4 = ((bf16[20,16,512]{2,1,0:T(8,128)(2,1)}), bf16[20,16,512]{2,1,0:T(8,128)(2,1)}, u32[]{:S(2)}, u32[]{:S(2)}) async-start(bf16[20,16,512]{2,1,0:T(8,128)(2,1)} %convert_element_type.102), calls=%async_computation.4 | async-start | bytes 655360 | tf_op jit(solution)/shard_map/all_to_all | solution.py:206
  623.8 20.5 %collective-permute-start.59 = (f32[512,8]{0,1:T(8,128)S(1)}, f32[512,8]{0,1:T(8,128)S(1)}, u32[]{:S(2)}, u32[]{:S(2)}) collective-permute-start(f32[512,8]{0,1:T(8,128)S(1)} %get-tuple-element.51), channel_id=1, source_target_pairs={{0,96},{4,100},{8,104},{12,108},{16,112},{20,116},{24,120},{28,124... | collective-permute-start | bytes 49160
  626.0 19.7 %collective-permute-start.58 = (f32[512,8]{0,1:T(8,128)S(1)}, f32[512,8]{0,1:T(8,128)}, u32[]{:S(2)}, u32[]{:S(2)}) collective-permute-start(f32[512,8]{0,1:T(8,128)S(1)} %get-tuple-element.51), channel_id=1, source_target_pairs={{0,92},{4,96},{8,100},{12,104},{16,108},{20,112},{24,116},{28,120}... | collective-permute-start | bytes 49160
  628.2 19.8 %collective-permute-start.57 = (f32[512,8]{0,1:T(8,128)S(1)}, f32[512,8]{0,1:T(8,128)}, u32[]{:S(2)}, u32[]{:S(2)}) collective-permute-start(f32[512,8]{0,1:T(8,128)S(1)} %get-tuple-element.51), channel_id=1, source_target_pairs={{0,88},{4,92},{8,96},{12,100},{16,104},{20,108},{24,112},{28,116},... | collective-permute-start | bytes 49160
  630.2 19.6 %collective-permute-start.56 = (f32[512,8]{0,1:T(8,128)S(1)}, f32[512,8]{0,1:T(8,128)}, u32[]{:S(2)}, u32[]{:S(2)}) collective-permute-start(f32[512,8]{0,1:T(8,128)S(1)} %get-tuple-element.51), channel_id=1, source_target_pairs={{0,84},{4,88},{8,92},{12,96},{16,100},{20,104},{24,108},{28,112},{... | collective-permute-start | bytes 49160
  632.2 19.8 %collective-permute-start.55 = (f32[512,8]{0,1:T(8,128)S(1)}, f32[512,8]{0,1:T(8,128)}, u32[]{:S(2)}, u32[]{:S(2)}) collective-permute-start(f32[512,8]{0,1:T(8,128)S(1)} %get-tuple-element.51), channel_id=1, source_target_pairs={{0,80},{4,84},{8,88},{12,92},{16,96},{20,100},{24,104},{28,108},{3... | collective-permute-start | bytes 49160
  637.2 50.3 %all-to-all-start.5 = ((bf16[20,16,512]{2,1,0:T(8,128)(2,1)}), bf16[20,16,512]{2,1,0:T(8,128)(2,1)S(1)}, u32[]{:S(2)}, u32[]{:S(2)}) async-start(bf16[20,16,512]{2,1,0:T(8,128)(2,1)} %convert_element_type.105), calls=%async_computation.5 | async-start | bytes 655360 | tf_op jit(solution)/shard_map/all_to_all | solution.py:207
  644.3 29.3 %collective-permute-start.54 = (f32[512,8]{0,1:T(8,128)S(1)}, f32[512,8]{0,1:T(8,128)S(1)}, u32[]{:S(2)}, u32[]{:S(2)}) collective-permute-start(f32[512,8]{0,1:T(8,128)S(1)} %get-tuple-element.51), channel_id=1, source_target_pairs={{0,76},{4,80},{8,84},{12,88},{16,92},{20,96},{24,100},{28,104},{32... | collective-permute-start | bytes 49160
  645.7 29.8 %collective-permute-start.53 = (f32[512,8]{0,1:T(8,128)S(1)}, f32[512,8]{0,1:T(8,128)S(1)}, u32[]{:S(2)}, u32[]{:S(2)}) collective-permute-start(f32[512,8]{0,1:T(8,128)S(1)} %get-tuple-element.51), channel_id=1, source_target_pairs={{0,72},{4,76},{8,80},{12,84},{16,88},{20,92},{24,96},{28,100},{32,... | collective-permute-start | bytes 49160
  648.0 29.5 %collective-permute-start.52 = (f32[512,8]{0,1:T(8,128)S(1)}, f32[512,8]{0,1:T(8,128)}, u32[]{:S(2)}, u32[]{:S(2)}) collective-permute-start(f32[512,8]{0,1:T(8,128)S(1)} %get-tuple-element.51), channel_id=1, source_target_pairs={{0,68},{4,72},{8,76},{12,80},{16,84},{20,88},{24,92},{28,96},{32,1... | collective-permute-start | bytes 49160
  649.9 29.9 %collective-permute-start.51 = (f32[512,8]{0,1:T(8,128)S(1)}, f32[512,8]{0,1:T(8,128)}, u32[]{:S(2)}, u32[]{:S(2)}) collective-permute-start(f32[512,8]{0,1:T(8,128)S(1)} %get-tuple-element.51), channel_id=1, source_target_pairs={{0,64},{4,68},{8,72},{12,76},{16,80},{20,84},{24,88},{28,92},{32,9... | collective-permute-start | bytes 49160
  652.0 30.0 %collective-permute-start.50 = (f32[512,8]{0,1:T(8,128)S(1)}, f32[512,8]{0,1:T(8,128)}, u32[]{:S(2)}, u32[]{:S(2)}) collective-permute-start(f32[512,8]{0,1:T(8,128)S(1)} %get-tuple-element.51), channel_id=1, source_target_pairs={{0,60},{4,64},{8,68},{12,72},{16,76},{20,80},{24,84},{28,88},{32,9... | collective-permute-start | bytes 49160
  673.6 21.0 %collective-permute-start.49 = (f32[512,8]{0,1:T(8,128)S(1)}, f32[512,8]{0,1:T(8,128)S(1)}, u32[]{:S(2)}, u32[]{:S(2)}) collective-permute-start(f32[512,8]{0,1:T(8,128)S(1)} %get-tuple-element.51), channel_id=1, source_target_pairs={{0,56},{4,60},{8,64},{12,68},{16,72},{20,76},{24,80},{28,84},{32,8... | collective-permute-start | bytes 49160
  675.5 22.5 %collective-permute-start.48 = (f32[512,8]{0,1:T(8,128)S(1)}, f32[512,8]{0,1:T(8,128)S(1)}, u32[]{:S(2)}, u32[]{:S(2)}) collective-permute-start(f32[512,8]{0,1:T(8,128)S(1)} %get-tuple-element.51), channel_id=1, source_target_pairs={{0,52},{4,56},{8,60},{12,64},{16,68},{20,72},{24,76},{28,80},{32,8... | collective-permute-start | bytes 49160
  677.5 23.7 %collective-permute-start.47 = (f32[512,8]{0,1:T(8,128)S(1)}, f32[512,8]{0,1:T(8,128)S(1)}, u32[]{:S(2)}, u32[]{:S(2)}) collective-permute-start(f32[512,8]{0,1:T(8,128)S(1)} %get-tuple-element.51), channel_id=1, source_target_pairs={{0,48},{4,52},{8,56},{12,60},{16,64},{20,68},{24,72},{28,76},{32,8... | collective-permute-start | bytes 49160
  679.8 23.4 %collective-permute-start.46 = (f32[512,8]{0,1:T(8,128)S(1)}, f32[512,8]{0,1:T(8,128)S(1)}, u32[]{:S(2)}, u32[]{:S(2)}) collective-permute-start(f32[512,8]{0,1:T(8,128)S(1)} %get-tuple-element.51), channel_id=1, source_target_pairs={{0,44},{4,48},{8,52},{12,56},{16,60},{20,64},{24,68},{28,72},{32,7... | collective-permute-start | bytes 49160
  682.0 24.8 %collective-permute-start.45 = (f32[512,8]{0,1:T(8,128)S(1)}, f32[512,8]{0,1:T(8,128)S(1)}, u32[]{:S(2)}, u32[]{:S(2)}) collective-permute-start(f32[512,8]{0,1:T(8,128)S(1)} %get-tuple-element.51), channel_id=1, source_target_pairs={{0,40},{4,44},{8,48},{12,52},{16,56},{20,60},{24,64},{28,68},{32,7... | collective-permute-start | bytes 49160
  687.5 65.1 %all-to-all-start.6 = ((bf16[20,16,512]{2,1,0:T(8,128)(2,1)}), bf16[20,16,512]{2,1,0:T(8,128)(2,1)S(1)}, u32[]{:S(2)}, u32[]{:S(2)}) async-start(bf16[20,16,512]{2,1,0:T(8,128)(2,1)} %convert_element_type.109), calls=%async_computation.6 | async-start | bytes 655360 | tf_op jit(solution)/shard_map/all_to_all | solution.py:208
  694.6 68.9 %reduce-scatter.7.cloned.1.call-start = ((), (), s32[]{:S(2)}) async-start(), calls=%async_computation.10 | async-start | bytes 20480 | tf_op jit(solution)/shard_map/reduce_scatter | solution.py:234
  694.6 24.8 %collective-permute-start.44 = (f32[512,8]{0,1:T(8,128)S(1)}, f32[512,8]{0,1:T(8,128)S(1)}, u32[]{:S(2)}, u32[]{:S(2)}) collective-permute-start(f32[512,8]{0,1:T(8,128)S(1)} %get-tuple-element.51), channel_id=1, source_target_pairs={{0,36},{4,40},{8,44},{12,48},{16,52},{20,56},{24,60},{28,64},{32,6... | collective-permute-start | bytes 49160
  698.1 27.4 %collective-permute-start.43 = (f32[512,8]{0,1:T(8,128)S(1)}, f32[512,8]{0,1:T(8,128)S(1)}, u32[]{:S(2)}, u32[]{:S(2)}) collective-permute-start(f32[512,8]{0,1:T(8,128)S(1)} %get-tuple-element.51), channel_id=1, source_target_pairs={{0,32},{4,36},{8,40},{12,44},{16,48},{20,52},{24,56},{28,60},{32,6... | collective-permute-start | bytes 49160
  701.2 26.2 %collective-permute-start.42 = (f32[512,8]{0,1:T(8,128)S(1)}, f32[512,8]{0,1:T(8,128)S(1)}, u32[]{:S(2)}, u32[]{:S(2)}) collective-permute-start(f32[512,8]{0,1:T(8,128)S(1)} %get-tuple-element.51), channel_id=1, source_target_pairs={{0,28},{4,32},{8,36},{12,40},{16,44},{20,48},{24,52},{28,56},{32,6... | collective-permute-start | bytes 49160
  703.2 26.2 %collective-permute-start.41 = (f32[512,8]{0,1:T(8,128)S(1)}, f32[512,8]{0,1:T(8,128)}, u32[]{:S(2)}, u32[]{:S(2)}) collective-permute-start(f32[512,8]{0,1:T(8,128)S(1)} %get-tuple-element.51), channel_id=1, source_target_pairs={{0,24},{4,28},{8,32},{12,36},{16,40},{20,44},{24,48},{28,52},{32,5... | collective-permute-start | bytes 49160
  706.7 24.6 %collective-permute-start.40 = (f32[512,8]{0,1:T(8,128)S(1)}, f32[512,8]{0,1:T(8,128)}, u32[]{:S(2)}, u32[]{:S(2)}) collective-permute-start(f32[512,8]{0,1:T(8,128)S(1)} %get-tuple-element.51), channel_id=1, source_target_pairs={{0,20},{4,24},{8,28},{12,32},{16,36},{20,40},{24,44},{28,48},{32,5... | collective-permute-start | bytes 49160
  719.4 29.9 %collective-permute-start.3 = (f32[5,15,512]{2,1,0:T(8,128)S(1)}, f32[5,15,512]{2,1,0:T(8,128)S(1)}, u32[]{:S(2)}, u32[]{:S(2)}) collective-permute-start(f32[5,15,512]{2,1,0:T(8,128)S(1)} %copy-done.31), channel_id=1, source_target_pairs={{4,0},{8,4},{12,8},{16,12},{20,16},{24,20},{28,24},{32,28},{36,32}... | collective-permute-start | bytes 460808 | tf_op jit(solution)/shard_map/ppermute | solution.py:14
  734.8 58.3 %reduce-scatter.9.cloned.1.call-start = ((), (), s32[]{:S(2)}) async-start(), calls=%async_computation.11 | async-start | bytes 20480 | tf_op jit(solution)/shard_map/reduce_scatter | solution.py:235
  (134 other events, 2682.7 us)
Sparse Core Ops, SparseCore 0:
  734.9 28.4 reduce-scatter.6
  767.0 25.9 reduce-scatter.8
where the time goes:
time: 810 us; the launch traced here: 800 us
  blocking collectives  317 us (39%)
  starting transfers between devices  283 us (35%)
  local copies, waits for them, and re-layouts  64.7 us (8%)
  waiting for transfers between devices  52.9 us (7%)
  matrix products  37.2 us (5%)
  other arithmetic  27.2 us (3%)
  between operations  17.5 us (2%)
    unnamed x1, blocking collectives  269 us
    unnamed x64, starting transfers between devices  206 us
    unnamed x223, local copies, waits for them, and re-layouts  35.6 us
    all_gather x1, blocking collectives, per_device(): lax.all_gather(out_time, 'series', axis=0, tiled=True)  30.3 us
    reduce_scatter x1, waiting for transfers between devices, per_device(): lax.psum_scatter(partial_sums[1], 'series', scatter_dimension=0, tiled=True)  29.6 us
    ppermute x4, starting transfers between devices, passed_along(): lax.ppermute(value, axis, [(source, source + steps) for source in range(l...  29.5 us
    all_gather x1, blocking collectives, per_device(): lax.all_gather(out_group, 'series', axis=0, tiled=True)  17.7 us
  transfers between devices with their start and end apart: 78, of which 9 were waited for; matrix products, arithmetic and copies ran while one was open for 49% of the time, Pallas kernels for 0%

commit v1 on v0

--- a/solution.py
+++ b/solution.py
@@ -157,7 +157,9 @@
     border_rows = BAND - 1
     w_time, w_group = (
         lax.all_gather(out_time, "series", axis=0, tiled=True),
-        lax.all_gather(out_group, "series", axis=0, tiled=True),
+        jnp.concatenate(
+            lax.all_to_all(jnp.stack([out_group] * lax.axis_size("series")), "series", 0, 0), axis=0
+        ),
     )
     cot_flat = cotangent.reshape(-1, cotangent.shape[2])
 

time: 810 us -> 815 us (level)
  blocking collectives: 317 us -> 299 us
  waiting for transfers between devices: 52.9 us -> 61.2 us
    all_gather x1 -> x0, blocking collectives: 17.7 us -> none  [per_device(): lax.all_gather(out_group, 'series', axis=0, tiled=True)]
    unnamed x223 -> x203, local copies, waits for them, and re-layouts: 35.6 us -> 36.4 us
  transfers between devices with their start and end apart: 78 -> 79, of which waited for: 9 -> 8; matrix products, arithmetic and copies ran while one was open for 49% -> 49% of each run, Pallas kernels for 0% -> 0%
where the time goes in v1:
time: 815 us; the launch traced here: 802 us
  blocking collectives  299 us (37%)
  starting transfers between devices  290 us (36%)
  local copies, waits for them, and re-layouts  67.6 us (8%)
  waiting for transfers between devices  61.2 us (8%)
  matrix products  40.5 us (5%)
  other arithmetic  26.9 us (3%)
  between operations  17.3 us (2%)
    unnamed x1, blocking collectives  270 us
    unnamed x64, starting transfers between devices  208 us
    unnamed x203, local copies, waits for them, and re-layouts  36.4 us
    reduce_scatter x1, waiting for transfers between devices, per_device(): lax.psum_scatter(partial_sums[1], 'series', scatter_dimension=0, tiled=True)  29.6 us
    all_gather x1, blocking collectives, per_device(): lax.all_gather(out_time, 'series', axis=0, tiled=True)  29.3 us
    ppermute x4, starting transfers between devices, passed_along(): lax.ppermute(value, axis, [(source, source + steps) for source in range(l...  28.3 us
  transfers between devices with their start and end apart: 79, of which 8 were waited for; matrix products, arithmetic and copies ran while one was open for 49% of the time, Pallas kernels for 0%

profile of v1, /device:TPU:2, one launch (start us, length us, event | category | flops | bytes accessed | tf_op | source)
XLA Modules:
  0.0 802.1 jit_solution(10565482842723886639)
XLA Ops:
  12.3 19.1 %collective-permute-start.1 = (bf16[5,15,512]{2,1,0:T(8,128)(2,1)}, bf16[5,15,512]{2,1,0:T(8,128)(2,1)}, u32[]{:S(2)}, u32[]{:S(2)}) collective-permute-start(bf16[5,15,512]{2,1,0:T(8,128)(2,1)} %slice.19), channel_id=1, source_target_pairs={{0,4},{4,8},{8,12},{12,16},{16,20},{20,24},{24,28},{28,32},{32,36}... | collective-permute-start | bytes 230408 | tf_op jit(solution)/shard_map/ppermute | solution.py:14
  33.3 8.7 %all-to-all-start.4 = ((bf16[5,64,512]{2,0,1:T(8,128)(2,1)}), bf16[5,64,512]{2,0,1:T(8,128)(2,1)S(1)}, u32[]{:S(2)}, u32[]{:S(2)}) async-start(bf16[5,64,512]{2,0,1:T(8,128)(2,1)} %copy.160), calls=%async_computation.4 | async-start | bytes 1048576 | tf_op jit(solution)/shard_map/all_to_all | solution.py:202
  43.2 29.3 %all_gather.3 = bf16[512,768]{1,0:T(8,128)(2,1)S(1)} all-gather(bf16[128,768]{1,0:T(8,128)(2,1)S(1)} %copy-done.23), channel_id=1, replica_groups=mesh['tm'=128,'series'=4] {'series'}, dimensions={0}, use_global_device_ids=true | all-gather | bytes 983040 | tf_op jit(solution)/shard_map/all_gather | solution.py:159
  72.5 4.7 all-to-all-start.1
  82.6 8.3 %all-to-all-done.1 = bf16[5,64,512]{2,0,1:T(8,128)(2,1)S(1)} async-done(((bf16[5,64,512]{2,0,1:T(8,128)(2,1)}), bf16[5,64,512]{2,0,1:T(8,128)(2,1)S(1)}, u32[]{:S(2)}, u32[]{:S(2)}) %all-to-all-start.1) | async-done | bytes 327712 | tf_op jit(solution)/shard_map/all_to_all | solution.py:201
  90.9 3.5 all-to-all-start
  102.0 4.2 all-to-all-done
  108.8 3.3 copy.156
  116.9 6.0 all-to-all-start.8
  127.2 5.4 all-to-all-done.8
  133.6 4.0 all-to-all-start.2
  140.1 3.6 fusion.34
  147.9 7.3 convolution_convert_fusion.5
  155.2 3.1 bitcast_multiply_fusion
  161.6 7.2 all-to-all-start.3
  168.8 269.5 %fusion.52 = (f32[512,8]{0,1:T(8,128)S(1)}, f32[512,8]{0,1:T(8,128)S(1)}) fusion(f32[512,768]{0,1:T(8,128)} %bitcast_multiply_fusion, f32[512,768]{0,1:T(8,128)} %convolution_multiply_fusion), kind=kCustom, calls=%all-reduce-scatter.2 | all-reduce-scatter fusion | flops 1048577 | bytes 3180544
  439.6 12.3 %collective-permute-start.33 = (f32[512,8]{0,1:T(8,128)S(1)}, f32[512,8]{0,1:T(8,128)S(1)}, u32[]{:S(2)}, u32[]{:S(2)}) collective-permute-start(f32[512,8]{0,1:T(8,128)S(1)} %get-tuple-element.50), channel_id=1, source_target_pairs={{0,120},{4,124},{8,128},{12,132},{16,136},{20,140},{24,144},{28,14... | collective-permute-start | bytes 49160
  451.9 7.8 collective-permute-start.32
  462.5 18.1 %collective-permute-start.31 = (f32[512,8]{0,1:T(8,128)S(1)}, f32[512,8]{0,1:T(8,128)S(1)}, u32[]{:S(2)}, u32[]{:S(2)}) collective-permute-start(f32[512,8]{0,1:T(8,128)S(1)} %get-tuple-element.50), channel_id=1, source_target_pairs={{0,112},{4,116},{8,120},{12,124},{16,128},{20,132},{24,136},{28,14... | collective-permute-start | bytes 49160
  480.6 10.9 %collective-permute-start.30 = (f32[512,8]{0,1:T(8,128)S(1)}, f32[512,8]{0,1:T(8,128)S(1)}, u32[]{:S(2)}, u32[]{:S(2)}) collective-permute-start(f32[512,8]{0,1:T(8,128)S(1)} %get-tuple-element.50), channel_id=1, source_target_pairs={{0,108},{4,112},{8,116},{12,120},{16,124},{20,128},{24,132},{28,13... | collective-permute-start | bytes 49160
  491.5 17.6 %collective-permute-start.29 = (f32[512,8]{0,1:T(8,128)S(1)}, f32[512,8]{0,1:T(8,128)S(1)}, u32[]{:S(2)}, u32[]{:S(2)}) collective-permute-start(f32[512,8]{0,1:T(8,128)S(1)} %get-tuple-element.50), channel_id=1, source_target_pairs={{0,104},{4,108},{8,112},{12,116},{16,120},{20,124},{24,128},{28,13... | collective-permute-start | bytes 49160
  511.1 3.1 collective-permute-start.27
  520.1 4.5 collective-permute-start.22
  531.7 3.8 collective-permute-start.18
  542.2 3.1 collective-permute-start.15
  547.9 3.0 collective-permute-start.13
  550.9 3.9 collective-permute-start.12
  555.9 4.2 collective-permute-start.11
  562.1 4.0 collective-permute-start.9
  566.1 3.9 collective-permute-start.8
  572.4 14.9 %fusion.10 = f32[16,8,20,20]{3,1,2,0:T(8,128)} fusion(bf16[16,8,20,20]{3,1,2,0:T(8,128)(2,1)S(1)} %copy.214, f32[16,8,20,20]{3,1,2,0:T(8,128)S(1)} %copy-done.8, f32[16,8,20]{1,2,0:T(8,128)S(1)} %copy-done.19), kind=kOutput, calls=%fused_computation.14 | output fusion | flops 412179 | bytes 522240 | tf_op jit(solution)/shard_map/sub | solution.py:26
  589.5 3.6 collective-permute-start.6
  606.0 5.1 all-to-all-start.5
  620.5 4.2 convolution_convert_fusion.4
  648.9 6.9 all-to-all-start.6
  655.9 7.4 fusion.45
  682.7 3.6 collective-permute-start.45
  688.6 3.4 collective-permute-start.44
  692.0 4.4 collective-permute-start.43
  698.4 4.3 collective-permute-start.41
  704.6 7.2 all-to-all-start.7
  712.8 9.6 %concatenate.16 = f32[512,262]{0,1:T(8,128)S(1)} concatenate(f32[512,6]{0,1:T(8,128)S(1)} %copy-done.33, f32[512,8]{0,1:T(8,128)S(1)} %collective-permute-done.34, f32[512,8]{0,1:T(8,128)S(1)} %copy-done.29, f32[512,8]{0,1:T(8,128)S(1)} %copy-done.31, f32[512,8]{0,1:T(8,128)S(1)} %copy-done.35, f32[512,8]{0,1:T(8,128)S(1)} %copy-done.37, f32[512,8]{0,1:T(8,128)S(1)} %copy-done.39, ...), dimensions={1} | concatenate | bytes 1073152
  722.4 5.4 collective-permute-start.3
  734.0 4.4 collective-permute-start.36
  739.6 3.7 collective-permute-done.36
  743.4 8.1 %concatenate.17 = f32[512,262]{0,1:T(8,128)S(1)} concatenate(f32[512,6]{0,1:T(8,128)S(1)} %collective-permute-done.67, f32[512,8]{0,1:T(8,128)S(1)} %copy-done.65, f32[512,8]{0,1:T(8,128)S(1)} %copy-done.67, f32[512,8]{0,1:T(8,128)S(1)} %copy-done.75, f32[512,8]{0,1:T(8,128)S(1)} %copy-done.79, f32[512,8]{0,1:T(8,128)S(1)} %copy-done.81, f32[512,8]{0,1:T(8,128)S(1)} %copy-done.83, ...), dimensions={1} | concatenate | bytes 1073152
  756.2 9.3 %reduce-scatter.7.cloned.1.call-done = f32[128,6]{0,1:T(8,128)} async-done(((f32[512,6]{0,1:T(8,128)}), f32[128,6]{0,1:T(8,128)}) %reduce-scatter.7.cloned.1.call-update) | async-done | bytes 3088 | tf_op jit(solution)/shard_map/reduce_scatter | solution.py:236
  765.5 29.6 %reduce-scatter.9.cloned.1.call-done = f32[128,6]{0,1:T(8,128)} async-done(((f32[512,6]{0,1:T(8,128)}), f32[128,6]{0,1:T(8,128)}) %reduce-scatter.9.cloned.1.call-update) | async-done | bytes 3088 | tf_op jit(solution)/shard_map/reduce_scatter | solution.py:237
  (382 shorter events, 162.6 us)
Async XLA Ops:
  8.8 85.5 %collective-permute-start = (bf16[5,15,512]{2,1,0:T(8,128)(2,1)}, bf16[5,15,512]{2,1,0:T(8,128)(2,1)}, u32[]{:S(2)}, u32[]{:S(2)}) collective-permute-start(bf16[5,15,512]{2,1,0:T(8,128)(2,1)} %slice.18), channel_id=1, source_target_pairs={{0,4},{4,8},{8,12},{12,16},{16,20},{20,24},{24,28},{28,32},{32,36}... | collective-permute-start | bytes 230408 | tf_op jit(solution)/shard_map/ppermute | solution.py:14
  12.3 84.3 %collective-permute-start.1 = (bf16[5,15,512]{2,1,0:T(8,128)(2,1)}, bf16[5,15,512]{2,1,0:T(8,128)(2,1)}, u32[]{:S(2)}, u32[]{:S(2)}) collective-permute-start(bf16[5,15,512]{2,1,0:T(8,128)(2,1)} %slice.19), channel_id=1, source_target_pairs={{0,4},{4,8},{8,12},{12,16},{16,20},{20,24},{24,28},{28,32},{32,36}... | collective-permute-start | bytes 230408 | tf_op jit(solution)/shard_map/ppermute | solution.py:14
  33.3 39.2 %all-to-all-start.4 = ((bf16[5,64,512]{2,0,1:T(8,128)(2,1)}), bf16[5,64,512]{2,0,1:T(8,128)(2,1)S(1)}, u32[]{:S(2)}, u32[]{:S(2)}) async-start(bf16[5,64,512]{2,0,1:T(8,128)(2,1)} %copy.160), calls=%async_computation.4 | async-start | bytes 1048576 | tf_op jit(solution)/shard_map/all_to_all | solution.py:202
  72.5 18.4 %all-to-all-start.1 = ((bf16[5,64,512]{2,0,1:T(8,128)(2,1)}), bf16[5,64,512]{2,0,1:T(8,128)(2,1)S(1)}, u32[]{:S(2)}, u32[]{:S(2)}) async-start(bf16[5,64,512]{2,0,1:T(8,128)(2,1)} %copy.152), calls=%async_computation.1 | async-start | bytes 1048576 | tf_op jit(solution)/shard_map/all_to_all | solution.py:201
  133.6 26.5 %all-to-all-start.2 = ((bf16[4,128,768]{2,1,0:T(8,128)(2,1)}), bf16[4,128,768]{2,1,0:T(8,128)(2,1)S(1)}, u32[]{:S(2)}, u32[]{:S(2)}) async-start(bf16[4,128,768]{2,1,0:T(8,128)(2,1)} %stack.2), calls=%async_computation.2 | async-start | bytes 1572864 | tf_op jit(solution)/shard_map/all_to_all | solution.py:161
  146.0 315.1 %collective-permute-start.2 = (f32[5,15,512]{2,1,0:T(8,128)}, f32[5,15,512]{2,1,0:T(8,128)S(1)}, u32[]{:S(2)}, u32[]{:S(2)}) collective-permute-start(f32[5,15,512]{2,1,0:T(8,128)} %copy.186), channel_id=1, source_target_pairs={{4,0},{8,4},{12,8},{16,12},{20,16},{24,20},{28,24},{32,28},{36,32}... | collective-permute-start | bytes 460808 | tf_op jit(solution)/shard_map/ppermute | solution.py:14
  161.6 378.1 %all-to-all-start.3 = ((bf16[5,64,512]{2,0,1:T(8,128)(2,1)}), bf16[5,64,512]{2,0,1:T(8,128)(2,1)S(1)}, u32[]{:S(2)}, u32[]{:S(2)}) async-start(bf16[5,64,512]{2,0,1:T(8,128)(2,1)} %copy.157), calls=%async_computation.3 | async-start | bytes 1048576 | tf_op jit(solution)/shard_map/all_to_all | solution.py:203
  438.3 53.2 %collective-permute-start.34 = (f32[512,8]{0,1:T(8,128)S(1)}, f32[512,8]{0,1:T(8,128)S(1)}, u32[]{:S(2)}, u32[]{:S(2)}) collective-permute-start(f32[512,8]{0,1:T(8,128)S(1)} %get-tuple-element.50), channel_id=1, source_target_pairs={{0,124},{4,128},{8,132},{12,136},{16,140},{20,144},{24,148},{28,15... | collective-permute-start | bytes 49160
  439.6 69.6 %collective-permute-start.33 = (f32[512,8]{0,1:T(8,128)S(1)}, f32[512,8]{0,1:T(8,128)S(1)}, u32[]{:S(2)}, u32[]{:S(2)}) collective-permute-start(f32[512,8]{0,1:T(8,128)S(1)} %get-tuple-element.50), channel_id=1, source_target_pairs={{0,120},{4,124},{8,128},{12,132},{16,136},{20,140},{24,144},{28,14... | collective-permute-start | bytes 49160
  451.9 59.2 %collective-permute-start.32 = (f32[512,8]{0,1:T(8,128)S(1)}, f32[512,8]{0,1:T(8,128)S(1)}, u32[]{:S(2)}, u32[]{:S(2)}) collective-permute-start(f32[512,8]{0,1:T(8,128)S(1)} %get-tuple-element.50), channel_id=1, source_target_pairs={{0,116},{4,120},{8,124},{12,128},{16,132},{20,136},{24,140},{28,14... | collective-permute-start | bytes 49160
  461.1 19.5 %collective-permute-start.67 = (f32[512,6]{0,1:T(8,128)S(1)}, f32[512,6]{0,1:T(8,128)S(1)}, u32[]{:S(2)}, u32[]{:S(2)}) collective-permute-start(f32[512,6]{0,1:T(8,128)S(1)} %slice.29), channel_id=1, source_target_pairs={{0,128},{4,132},{8,136},{12,140},{16,144},{20,148},{24,152},{28,15... | collective-permute-start | bytes 36872
  462.5 51.7 %collective-permute-start.31 = (f32[512,8]{0,1:T(8,128)S(1)}, f32[512,8]{0,1:T(8,128)S(1)}, u32[]{:S(2)}, u32[]{:S(2)}) collective-permute-start(f32[512,8]{0,1:T(8,128)S(1)} %get-tuple-element.50), channel_id=1, source_target_pairs={{0,112},{4,116},{8,120},{12,124},{16,128},{20,132},{24,136},{28,14... | collective-permute-start | bytes 49160
  480.6 35.0 %collective-permute-start.30 = (f32[512,8]{0,1:T(8,128)S(1)}, f32[512,8]{0,1:T(8,128)S(1)}, u32[]{:S(2)}, u32[]{:S(2)}) collective-permute-start(f32[512,8]{0,1:T(8,128)S(1)} %get-tuple-element.50), channel_id=1, source_target_pairs={{0,108},{4,112},{8,116},{12,120},{16,124},{20,128},{24,132},{28,13... | collective-permute-start | bytes 49160
  491.5 25.3 %collective-permute-start.29 = (f32[512,8]{0,1:T(8,128)S(1)}, f32[512,8]{0,1:T(8,128)S(1)}, u32[]{:S(2)}, u32[]{:S(2)}) collective-permute-start(f32[512,8]{0,1:T(8,128)S(1)} %get-tuple-element.50), channel_id=1, source_target_pairs={{0,104},{4,108},{8,112},{12,116},{16,120},{20,124},{24,128},{28,13... | collective-permute-start | bytes 49160
  531.7 16.2 %collective-permute-start.18 = (f32[512,8]{0,1:T(8,128)S(1)}, f32[512,8]{0,1:T(8,128)}, u32[]{:S(2)}, u32[]{:S(2)}) collective-permute-start(f32[512,8]{0,1:T(8,128)S(1)} %get-tuple-element.50), channel_id=1, source_target_pairs={{0,60},{4,64},{8,68},{12,72},{16,76},{20,80},{24,84},{28,88},{32,9... | collective-permute-start | bytes 49160
  542.2 17.9 %collective-permute-start.15 = (f32[512,8]{0,1:T(8,128)S(1)}, f32[512,8]{0,1:T(8,128)S(1)}, u32[]{:S(2)}, u32[]{:S(2)}) collective-permute-start(f32[512,8]{0,1:T(8,128)S(1)} %get-tuple-element.50), channel_id=1, source_target_pairs={{0,48},{4,52},{8,56},{12,60},{16,64},{20,68},{24,72},{28,76},{32,8... | collective-permute-start | bytes 49160
  545.3 16.8 %collective-permute-start.14 = (f32[512,8]{0,1:T(8,128)S(1)}, f32[512,8]{0,1:T(8,128)S(1)}, u32[]{:S(2)}, u32[]{:S(2)}) collective-permute-start(f32[512,8]{0,1:T(8,128)S(1)} %get-tuple-element.50), channel_id=1, source_target_pairs={{0,44},{4,48},{8,52},{12,56},{16,60},{20,64},{24,68},{28,72},{32,7... | collective-permute-start | bytes 49160
  547.9 18.2 %collective-permute-start.13 = (f32[512,8]{0,1:T(8,128)S(1)}, f32[512,8]{0,1:T(8,128)S(1)}, u32[]{:S(2)}, u32[]{:S(2)}) collective-permute-start(f32[512,8]{0,1:T(8,128)S(1)} %get-tuple-element.50), channel_id=1, source_target_pairs={{0,40},{4,44},{8,48},{12,52},{16,56},{20,60},{24,64},{28,68},{32,7... | collective-permute-start | bytes 49160
  550.9 19.1 %collective-permute-start.12 = (f32[512,8]{0,1:T(8,128)S(1)}, f32[512,8]{0,1:T(8,128)S(1)}, u32[]{:S(2)}, u32[]{:S(2)}) collective-permute-start(f32[512,8]{0,1:T(8,128)S(1)} %get-tuple-element.50), channel_id=1, source_target_pairs={{0,36},{4,40},{8,44},{12,48},{16,52},{20,56},{24,60},{28,64},{32,6... | collective-permute-start | bytes 49160
  555.9 33.6 %collective-permute-start.11 = (f32[512,8]{0,1:T(8,128)S(1)}, f32[512,8]{0,1:T(8,128)S(1)}, u32[]{:S(2)}, u32[]{:S(2)}) collective-permute-start(f32[512,8]{0,1:T(8,128)S(1)} %get-tuple-element.50), channel_id=1, source_target_pairs={{0,32},{4,36},{8,40},{12,44},{16,48},{20,52},{24,56},{28,60},{32,6... | collective-permute-start | bytes 49160
  560.1 32.9 %collective-permute-start.10 = (f32[512,8]{0,1:T(8,128)S(1)}, f32[512,8]{0,1:T(8,128)S(1)}, u32[]{:S(2)}, u32[]{:S(2)}) collective-permute-start(f32[512,8]{0,1:T(8,128)S(1)} %get-tuple-element.50), channel_id=1, source_target_pairs={{0,28},{4,32},{8,36},{12,40},{16,44},{20,48},{24,52},{28,56},{32,6... | collective-permute-start | bytes 49160
  562.1 32.9 %collective-permute-start.9 = (f32[512,8]{0,1:T(8,128)S(1)}, f32[512,8]{0,1:T(8,128)S(1)}, u32[]{:S(2)}, u32[]{:S(2)}) collective-permute-start(f32[512,8]{0,1:T(8,128)S(1)} %get-tuple-element.50), channel_id=1, source_target_pairs={{0,24},{4,28},{8,32},{12,36},{16,40},{20,44},{24,48},{28,52},{32,5... | collective-permute-start | bytes 49160
  566.1 31.1 %collective-permute-start.8 = (f32[512,8]{0,1:T(8,128)S(1)}, f32[512,8]{0,1:T(8,128)S(1)}, u32[]{:S(2)}, u32[]{:S(2)}) collective-permute-start(f32[512,8]{0,1:T(8,128)S(1)} %get-tuple-element.50), channel_id=1, source_target_pairs={{0,20},{4,24},{8,28},{12,32},{16,36},{20,40},{24,44},{28,48},{32,5... | collective-permute-start | bytes 49160
  570.0 28.5 %collective-permute-start.7 = (f32[512,8]{0,1:T(8,128)S(1)}, f32[512,8]{0,1:T(8,128)}, u32[]{:S(2)}, u32[]{:S(2)}) collective-permute-start(f32[512,8]{0,1:T(8,128)S(1)} %get-tuple-element.50), channel_id=1, source_target_pairs={{0,16},{4,20},{8,24},{12,28},{16,32},{20,36},{24,40},{28,44},{32,4... | collective-permute-start | bytes 49160
  589.5 21.5 %collective-permute-start.6 = (f32[512,8]{0,1:T(8,128)S(1)}, f32[512,8]{0,1:T(8,128)}, u32[]{:S(2)}, u32[]{:S(2)}) collective-permute-start(f32[512,8]{0,1:T(8,128)S(1)} %get-tuple-element.50), channel_id=1, source_target_pairs={{0,12},{4,16},{8,20},{12,24},{16,28},{20,32},{24,36},{28,40},{32,4... | collective-permute-start | bytes 49160
  593.1 19.7 %collective-permute-start.5 = (f32[512,8]{0,1:T(8,128)S(1)}, f32[512,8]{0,1:T(8,128)}, u32[]{:S(2)}, u32[]{:S(2)}) collective-permute-start(f32[512,8]{0,1:T(8,128)S(1)} %get-tuple-element.50), channel_id=1, source_target_pairs={{0,8},{4,12},{8,16},{12,20},{16,24},{20,28},{24,32},{28,36},{32,40... | collective-permute-start | bytes 49160
  595.0 19.8 %collective-permute-start.4 = (f32[512,8]{0,1:T(8,128)S(1)}, f32[512,8]{0,1:T(8,128)}, u32[]{:S(2)}, u32[]{:S(2)}) collective-permute-start(f32[512,8]{0,1:T(8,128)S(1)} %get-tuple-element.50), channel_id=1, source_target_pairs={{0,4},{4,8},{8,12},{12,16},{16,20},{20,24},{24,28},{28,32},{32,36}... | collective-permute-start | bytes 49160
  597.2 19.2 %collective-permute-start.66 = (f32[512,8]{0,1:T(8,128)S(1)}, f32[512,8]{0,1:T(8,128)S(1)}, u32[]{:S(2)}, u32[]{:S(2)}) collective-permute-start(f32[512,8]{0,1:T(8,128)S(1)} %get-tuple-element.51), channel_id=1, source_target_pairs={{0,124},{4,128},{8,132},{12,136},{16,140},{20,144},{24,148},{28,15... | collective-permute-start | bytes 49160
  598.5 20.0 %collective-permute-start.65 = (f32[512,8]{0,1:T(8,128)S(1)}, f32[512,8]{0,1:T(8,128)S(1)}, u32[]{:S(2)}, u32[]{:S(2)}) collective-permute-start(f32[512,8]{0,1:T(8,128)S(1)} %get-tuple-element.51), channel_id=1, source_target_pairs={{0,120},{4,124},{8,128},{12,132},{16,136},{20,140},{24,144},{28,14... | collective-permute-start | bytes 49160
  606.0 42.9 %all-to-all-start.5 = ((bf16[20,16,512]{2,1,0:T(8,128)(2,1)}), bf16[20,16,512]{2,1,0:T(8,128)(2,1)}, u32[]{:S(2)}, u32[]{:S(2)}) async-start(bf16[20,16,512]{2,1,0:T(8,128)(2,1)} %convert_element_type.102), calls=%async_computation.5 | async-start | bytes 655360 | tf_op jit(solution)/shard_map/all_to_all | solution.py:208
  638.1 36.5 %collective-permute-start.54 = (f32[512,8]{0,1:T(8,128)S(1)}, f32[512,8]{0,1:T(8,128)}, u32[]{:S(2)}, u32[]{:S(2)}) collective-permute-start(f32[512,8]{0,1:T(8,128)S(1)} %get-tuple-element.51), channel_id=1, source_target_pairs={{0,76},{4,80},{8,84},{12,88},{16,92},{20,96},{24,100},{28,104},{32... | collective-permute-start | bytes 49160
  640.0 36.6 %collective-permute-start.53 = (f32[512,8]{0,1:T(8,128)S(1)}, f32[512,8]{0,1:T(8,128)}, u32[]{:S(2)}, u32[]{:S(2)}) collective-permute-start(f32[512,8]{0,1:T(8,128)S(1)} %get-tuple-element.51), channel_id=1, source_target_pairs={{0,72},{4,76},{8,80},{12,84},{16,88},{20,92},{24,96},{28,100},{32,... | collective-permute-start | bytes 49160
  642.2 36.3 %collective-permute-start.52 = (f32[512,8]{0,1:T(8,128)S(1)}, f32[512,8]{0,1:T(8,128)}, u32[]{:S(2)}, u32[]{:S(2)}) collective-permute-start(f32[512,8]{0,1:T(8,128)S(1)} %get-tuple-element.51), channel_id=1, source_target_pairs={{0,68},{4,72},{8,76},{12,80},{16,84},{20,88},{24,92},{28,96},{32,1... | collective-permute-start | bytes 49160
  644.0 36.5 %collective-permute-start.51 = (f32[512,8]{0,1:T(8,128)S(1)}, f32[512,8]{0,1:T(8,128)}, u32[]{:S(2)}, u32[]{:S(2)}) collective-permute-start(f32[512,8]{0,1:T(8,128)S(1)} %get-tuple-element.51), channel_id=1, source_target_pairs={{0,64},{4,68},{8,72},{12,76},{16,80},{20,84},{24,88},{28,92},{32,9... | collective-permute-start | bytes 49160
  646.0 36.8 %collective-permute-start.50 = (f32[512,8]{0,1:T(8,128)S(1)}, f32[512,8]{0,1:T(8,128)}, u32[]{:S(2)}, u32[]{:S(2)}) collective-permute-start(f32[512,8]{0,1:T(8,128)S(1)} %get-tuple-element.51), channel_id=1, source_target_pairs={{0,60},{4,64},{8,68},{12,72},{16,76},{20,80},{24,84},{28,88},{32,9... | collective-permute-start | bytes 49160
  648.9 55.7 %all-to-all-start.6 = ((bf16[20,16,512]{2,1,0:T(8,128)(2,1)}), bf16[20,16,512]{2,1,0:T(8,128)(2,1)S(1)}, u32[]{:S(2)}, u32[]{:S(2)}) async-start(bf16[20,16,512]{2,1,0:T(8,128)(2,1)} %convert_element_type.105), calls=%async_computation.6 | async-start | bytes 655360 | tf_op jit(solution)/shard_map/all_to_all | solution.py:209
  678.5 17.9 %collective-permute-start.47 = (f32[512,8]{0,1:T(8,128)S(1)}, f32[512,8]{0,1:T(8,128)S(1)}, u32[]{:S(2)}, u32[]{:S(2)}) collective-permute-start(f32[512,8]{0,1:T(8,128)S(1)} %get-tuple-element.51), channel_id=1, source_target_pairs={{0,48},{4,52},{8,56},{12,60},{16,64},{20,68},{24,72},{28,76},{32,8... | collective-permute-start | bytes 49160
  680.5 17.8 %collective-permute-start.46 = (f32[512,8]{0,1:T(8,128)S(1)}, f32[512,8]{0,1:T(8,128)S(1)}, u32[]{:S(2)}, u32[]{:S(2)}) collective-permute-start(f32[512,8]{0,1:T(8,128)S(1)} %get-tuple-element.51), channel_id=1, source_target_pairs={{0,44},{4,48},{8,52},{12,56},{16,60},{20,64},{24,68},{28,72},{32,7... | collective-permute-start | bytes 49160
  682.7 19.9 %collective-permute-start.45 = (f32[512,8]{0,1:T(8,128)S(1)}, f32[512,8]{0,1:T(8,128)S(1)}, u32[]{:S(2)}, u32[]{:S(2)}) collective-permute-start(f32[512,8]{0,1:T(8,128)S(1)} %get-tuple-element.51), channel_id=1, source_target_pairs={{0,40},{4,44},{8,48},{12,52},{16,56},{20,60},{24,64},{28,68},{32,7... | collective-permute-start | bytes 49160
  688.6 33.8 %collective-permute-start.44 = (f32[512,8]{0,1:T(8,128)S(1)}, f32[512,8]{0,1:T(8,128)S(1)}, u32[]{:S(2)}, u32[]{:S(2)}) collective-permute-start(f32[512,8]{0,1:T(8,128)S(1)} %get-tuple-element.51), channel_id=1, source_target_pairs={{0,36},{4,40},{8,44},{12,48},{16,52},{20,56},{24,60},{28,64},{32,6... | collective-permute-start | bytes 49160
  692.0 35.8 %collective-permute-start.43 = (f32[512,8]{0,1:T(8,128)S(1)}, f32[512,8]{0,1:T(8,128)S(1)}, u32[]{:S(2)}, u32[]{:S(2)}) collective-permute-start(f32[512,8]{0,1:T(8,128)S(1)} %get-tuple-element.51), channel_id=1, source_target_pairs={{0,32},{4,36},{8,40},{12,44},{16,48},{20,52},{24,56},{28,60},{32,6... | collective-permute-start | bytes 49160
  696.4 33.3 %collective-permute-start.42 = (f32[512,8]{0,1:T(8,128)S(1)}, f32[512,8]{0,1:T(8,128)S(1)}, u32[]{:S(2)}, u32[]{:S(2)}) collective-permute-start(f32[512,8]{0,1:T(8,128)S(1)} %get-tuple-element.51), channel_id=1, source_target_pairs={{0,28},{4,32},{8,36},{12,40},{16,44},{20,48},{24,52},{28,56},{32,6... | collective-permute-start | bytes 49160
  698.4 33.5 %collective-permute-start.41 = (f32[512,8]{0,1:T(8,128)S(1)}, f32[512,8]{0,1:T(8,128)S(1)}, u32[]{:S(2)}, u32[]{:S(2)}) collective-permute-start(f32[512,8]{0,1:T(8,128)S(1)} %get-tuple-element.51), channel_id=1, source_target_pairs={{0,24},{4,28},{8,32},{12,36},{16,40},{20,44},{24,48},{28,52},{32,5... | collective-permute-start | bytes 49160
  702.7 31.3 %collective-permute-start.40 = (f32[512,8]{0,1:T(8,128)S(1)}, f32[512,8]{0,1:T(8,128)S(1)}, u32[]{:S(2)}, u32[]{:S(2)}) collective-permute-start(f32[512,8]{0,1:T(8,128)S(1)} %get-tuple-element.51), channel_id=1, source_target_pairs={{0,20},{4,24},{8,28},{12,32},{16,36},{20,40},{24,44},{28,48},{32,5... | collective-permute-start | bytes 49160
  704.6 50.8 %all-to-all-start.7 = ((bf16[20,16,512]{2,1,0:T(8,128)(2,1)}), bf16[20,16,512]{2,1,0:T(8,128)(2,1)S(1)}, u32[]{:S(2)}, u32[]{:S(2)}) async-start(bf16[20,16,512]{2,1,0:T(8,128)(2,1)} %convert_element_type.109), calls=%async_computation.7 | async-start | bytes 655360 | tf_op jit(solution)/shard_map/all_to_all | solution.py:210
  711.8 53.6 %reduce-scatter.7.cloned.1.call-start = ((), (), s32[]{:S(2)}) async-start(), calls=%async_computation.11 | async-start | bytes 20480 | tf_op jit(solution)/shard_map/reduce_scatter | solution.py:236
  722.4 29.7 %collective-permute-start.3 = (f32[5,15,512]{2,1,0:T(8,128)S(1)}, f32[5,15,512]{2,1,0:T(8,128)S(1)}, u32[]{:S(2)}, u32[]{:S(2)}) collective-permute-start(f32[5,15,512]{2,1,0:T(8,128)S(1)} %copy-done.27), channel_id=1, source_target_pairs={{4,0},{8,4},{12,8},{16,12},{20,16},{24,20},{28,24},{32,28},{36,32}... | collective-permute-start | bytes 460808 | tf_op jit(solution)/shard_map/ppermute | solution.py:14
  739.1 56.0 %reduce-scatter.9.cloned.1.call-start = ((), (), s32[]{:S(2)}) async-start(), calls=%async_computation.12 | async-start | bytes 20480 | tf_op jit(solution)/shard_map/reduce_scatter | solution.py:237
  (125 other events, 2507.7 us)
Sparse Core Ops, SparseCore 0:
  739.2 26.2 reduce-scatter.6
  769.0 25.9 reduce-scatter.8
